TPU v7x, 32 devices: a whole 2x2x4 slice. The times are simulated.
32 devices in a mesh: groups: 2 (over x), tensor: 16 (over z, y, core).
Axes of the slice: x: 2, y: 2, z: 4, core: 2. Of those that a mesh axis runs over, the one named last changes fastest.
Arguments:
- input_rows: bfloat16 [512, 8192], P(('groups', 'tensor')), parts along dimension 0, may hold values from -6 to 6
- up_weight: bfloat16 [8192, 28672], P(None, 'tensor'), may hold values from -0.0625 to 0.0625
- adapter_down: bfloat16 [32, 64, 8192], P(('groups', 'tensor')), parts along dimension 0, may hold values from -0.0625 to 0.0625
- adapter_up: bfloat16 [32, 64, 28672], P(('groups', 'tensor')), parts along dimension 0, may hold values from -0.75 to 0.75
- ranks: int32 [32], P('groups'), parts along dimension 0, may hold values from 16 to 64, as said below
- adapter_slot: int32 [32], P('groups'), parts along dimension 0, may hold values from 0 to 15, each once
- segment_lengths: int32 [32], P('groups'), parts along dimension 0, may hold values from 1 to 64, 256 in all
- segment_adapter: int32 [32], P('groups'), parts along dimension 0, may hold values from 0 to 15
Outputs:
- up_out: bfloat16 [512, 28672], P('groups', 'tensor'), parts along dimension 0
There are 2 independent parts, one for each index of `groups`. A program takes and returns all parts, laid end to end along the dimension named above; an argument that names none is the same for every part. Nothing has to cross between parts.
Inputs may be any that keep to these rules, and one draw needn't show every extreme that they name: `ranks`: a multiple of 16; the columns j >= the rank of an adapter's 64 are unused. `adapter_slot`: each storage slot holds exactly one adapter. `segment_lengths`: the segments sum to 256.
All inputs are finite; a program needn't handle non-finite values.
Results may differ from a plain program's by a relative error of at most 0.0039.
Values may be sent and summed in bfloat16 or wider, within the bound.
No kernel may reach another device: no remote copies, remote signals or barrier semaphores. Data moves between devices by JAX's collectives and lax.ppermute only.
A program may use at most 128 MiB of HBM per device.

v0:
```python
import math

import jax
import jax.numpy as jnp
from jax import lax
from jax.sharding import PartitionSpec as P

ADAPTER_ALPHA = 32.0


def row_tables(row_count, ranks, adapter_slot, segment_lengths, segment_adapter):
    seg_ends = jnp.cumsum(segment_lengths)
    positions = jnp.arange(row_count, dtype=jnp.int32)
    seg_row = jnp.sum((seg_ends[None, :] <= positions[:, None]).astype(jnp.int32), axis=1)
    seg_pick = (
        seg_row[:, None] == jnp.arange(segment_lengths.shape[0], dtype=jnp.int32)[None, :]
    ).astype(jnp.int32)
    adapter_row = jnp.sum(seg_pick * segment_adapter[None, :], axis=1)
    pool_pick = (
        adapter_row[:, None] == jnp.arange(ranks.shape[0], dtype=jnp.int32)[None, :]
    ).astype(jnp.int32)
    slot_row = jnp.sum(pool_pick * adapter_slot[None, :], axis=1)
    row_rank_values = jnp.sum(pool_pick * ranks[None, :], axis=1)
    return (slot_row, row_rank_values)


def coefficients(shrink, row_rank_values):
    columns = jnp.arange(shrink.shape[1], dtype=jnp.int32)
    row_scale_values = ADAPTER_ALPHA / row_rank_values.astype(jnp.float32)
    inside = columns[None, :] < row_rank_values[:, None]
    return jnp.where(inside, shrink * row_scale_values[:, None], jnp.zeros_like(shrink)).astype(
        jnp.bfloat16
    )


def on_device(
    input_rows,
    up_weight,
    adapter_down,
    adapter_up,
    ranks,
    adapter_slot,
    segment_lengths,
    segment_adapter,
):
    shards = lax.axis_size("tensor")
    position = lax.axis_index("tensor")
    total_rows = input_rows.shape[0] * shards
    slot_row, row_rank_values = row_tables(
        total_rows, ranks, adapter_slot, segment_lengths, segment_adapter
    )
    pool_size = ranks.shape[0]
    up_factor_slices = lax.all_to_all(adapter_up, "tensor", split_axis=2, concat_axis=0, tiled=True)
    segment_piece = lax.all_gather(input_rows, "tensor", axis=0, tiled=True)
    base_part = jnp.dot(segment_piece, up_weight, preferred_element_type=jnp.float32)
    stored_factor = adapter_down.shape[0]
    local_slot = slot_row - position * stored_factor
    rank_product = jnp.einsum(
        "gf,ouf->gou", segment_piece, adapter_down, preferred_element_type=jnp.float32
    )
    owned = (local_slot[:, None] == jnp.arange(stored_factor, dtype=jnp.int32)[None, :]).astype(
        jnp.float32
    )
    combined = jnp.concatenate(
        [base_part, jnp.sum(rank_product * owned[:, :, None], axis=1)], axis=1
    )
    hidden_width = up_weight.shape[1]
    base = combined[:, :hidden_width]
    shrink = lax.psum(combined[:, hidden_width:], "tensor")
    coeff = coefficients(shrink, row_rank_values)
    rank_width = coeff.shape[1]
    row_block = math.gcd(total_rows, 256)
    coeff_blocks = coeff.reshape(total_rows // row_block, row_block, rank_width)
    slot_blocks = slot_row.reshape(total_rows // row_block, row_block)
    flat_up = up_factor_slices.reshape(pool_size * rank_width, hidden_width)
    pool_ids = jnp.arange(pool_size, dtype=jnp.int32)

    def expand(item):
        block_coeff, block_slots = item
        picked = (block_slots[:, None] == pool_ids[None, :]).astype(jnp.bfloat16)
        placed = (picked[:, :, None] * block_coeff[:, None, :]).reshape(
            row_block, pool_size * rank_width
        )
        placed = lax.optimization_barrier(placed)
        return jnp.dot(placed, flat_up, preferred_element_type=jnp.float32)

    adapter_term = lax.map(expand, (coeff_blocks, slot_blocks)).reshape(total_rows, hidden_width)
    return (base + adapter_term).astype(jnp.bfloat16)


def solution(mesh):
    placed = (
        P(("groups", "tensor"), None),
        P(None, "tensor"),
        P(("groups", "tensor"), None, None),
        P(("groups", "tensor"), None, None),
        P("groups"),
        P("groups"),
        P("groups"),
        P("groups"),
    )
    return jax.shard_map(
        on_device, mesh=mesh, in_specs=placed, out_specs=P("groups", "tensor"), check_vma=False
    )
```

profile of v0, /device:TPU:0, one launch (start us, length us, event | category | flops | bytes accessed | tf_op | source)
XLA Modules:
  0.0 445.1 jit_solution(15900713807419762448)
XLA Ops:
  6.5 0.0 copy-start
  6.5 0.0 all-gather.2.cloned.1.call-start
  6.5 0.7 all-gather.2.cloned.1.call-update
  7.3 29.0 %copy.19 = bf16[1,64,28672]{1,0,2:T(2,128)(2,1)} copy(bf16[1,64,28672]{2,1,0:T(8,128)(2,1)} %param.11) | data formatting | bytes 7340032 | tf_op args[3]
  36.3 0.5 broadcast.50
  36.8 157.2 %reduce.1 = bf16[28672,64]{1,0:T(8,128)(2,1)} reduce(bf16[28672,1,64]{2,1,0:T(2,128)(2,1)} %bitcast.21, bf16[]{:T(256)} %broadcast.50), dimensions={1}, to_apply=%bitcast.13.reduce_sub_computation | reduce | bytes 7340034
  194.0 13.3 %reshape.98 = bf16[16,2,57344]{2,1,0:T(2,128)(2,1)} reshape(bf16[28672,64]{1,0:T(8,128)(2,1)} %reduce.1) | data formatting | bytes 7340032
  207.3 0.0 copy-start.1
  207.3 7.4 %all-to-all-start = ((bf16[16,2,57344]{2,1,0:T(2,128)(2,1)}), bf16[16,2,57344]{2,1,0:T(2,128)(2,1)}, u32[]{:S(2)}, u32[]{:S(2)}) async-start(bf16[16,2,57344]{2,1,0:T(2,128)(2,1)} %reshape.98), calls=%async_computation | async-start | bytes 7340032 | tf_op jit(solution)/shard_map/all_to_all | solution.py:53
  214.8 0.2 all-reduce.2.cloned.1.call-start
  215.0 0.0 copy-done.1
  215.0 0.1 copy.18
  215.1 0.1 reduce
  215.3 0.1 convert_reduce_fusion
  215.3 0.0 copy-done.2
  215.4 0.1 select_reduce_fusion.2
  215.4 0.0 copy-done.3
  215.4 0.0 copy-done.4
  215.4 0.1 select_reduce_fusion
  215.6 67.8 %all-to-all-done = bf16[16,2,57344]{2,1,0:T(2,128)(2,1)} async-done(((bf16[16,2,57344]{2,1,0:T(2,128)(2,1)}), bf16[16,2,57344]{2,1,0:T(2,128)(2,1)}, u32[]{:S(2)}, u32[]{:S(2)}) %all-to-all-start) | async-done | bytes 3670048 | tf_op jit(solution)/shard_map/all_to_all | solution.py:53
  283.3 14.2 %reshape.99 = bf16[28672,1,64]{2,1,0:T(2,128)(2,1)} reshape(bf16[16,2,57344]{2,1,0:T(2,128)(2,1)} %all-to-all-done) | data formatting | bytes 7340032
  297.5 28.0 %copy.20 = bf16[1,64,28672]{2,1,0:T(8,128)(2,1)} copy(bf16[1,64,28672]{1,0,2:T(2,128)(2,1)} %bitcast.22) | data formatting | bytes 7340032 | tf_op jit(solution)/shard_map/all_to_all | solution.py:53
  325.6 2.8 copy.22
  328.3 0.2 bitcast_bitcast_fusion
  328.6 2.9 copy.21
  331.5 0.0 copy-done
  331.5 4.2 convolution_multiply_fusion
  335.7 0.0 all-reduce.2.cloned.1.call-update
  335.7 15.4 %fusion.3 = f32[256,1792]{1,0:T(8,128)S(1)} fusion(bf16[256,8192]{1,0:T(8,128)(2,1)} %all-gather.2.cloned.1.call-done, bf16[8192,1792]{1,0:T(8,128)(2,1)} %param.9), kind=kOutput, calls=%fused_computation.19 | convolution fusion | flops 7516192768 | bytes 35389440 | tf_op jit(solution)/shard_map/dot_general | solution.py:55
  351.2 82.1 %all-reduce.2.cloned.1.call-done = f32[256,64]{0,1:T(8,128)} async-done(((f32[256,64]{0,1:T(8,128)}), f32[256,64]{0,1:T(8,128)}) %all-reduce.2.cloned.1.call-update) | async-done | bytes 65552 | tf_op jit(solution)/shard_map/psum | solution.py:69
  433.2 0.9 select_convert_fusion
  434.1 4.1 fusion
  (9 shorter events, 0.1 us)
Async XLA Ops:
  6.5 324.9 %copy-start = (bf16[1,64,8192]{2,1,0:T(8,128)(2,1)S(1)}, bf16[1,64,8192]{2,1,0:T(8,128)(2,1)}, u32[]{:S(2)}) copy-start(bf16[1,64,8192]{2,1,0:T(8,128)(2,1)} %param.10) | copy-start | bytes 3145732
  6.5 324.9 %all-gather.2.cloned.1.call-start = ((), (), s32[]{:S(2)}) async-start(), calls=%async_computation.1 | async-start | bytes 4456448 | tf_op jit(solution)/shard_map/all_gather | solution.py:54
  207.3 7.7 %copy-start.1 = (s32[16]{0:T(128)S(1)}, s32[16]{0:T(128)}, u32[]{:S(2)}) copy-start(s32[16]{0:T(128)} %param.14) | copy-start | bytes 196
  207.3 8.0 %copy-start.2 = (s32[16]{0:T(128)S(1)}, s32[16]{0:T(128)}, u32[]{:S(2)}) copy-start(s32[16]{0:T(128)} %param.15) | copy-start | bytes 196
  207.3 8.1 %copy-start.3 = (s32[16]{0:T(128)S(1)}, s32[16]{0:T(128)}, u32[]{:S(2)}) copy-start(s32[16]{0:T(128)} %param.12) | copy-start | bytes 196
  207.3 8.1 %copy-start.4 = (s32[16]{0:T(128)S(1)}, s32[16]{0:T(128)}, u32[]{:S(2)}) copy-start(s32[16]{0:T(128)} %param.13) | copy-start | bytes 196
  207.3 76.0 %all-to-all-start = ((bf16[16,2,57344]{2,1,0:T(2,128)(2,1)}), bf16[16,2,57344]{2,1,0:T(2,128)(2,1)}, u32[]{:S(2)}, u32[]{:S(2)}) async-start(bf16[16,2,57344]{2,1,0:T(2,128)(2,1)} %reshape.98), calls=%async_computation | async-start | bytes 7340032 | tf_op jit(solution)/shard_map/all_to_all | solution.py:53
  214.8 218.4 %all-reduce.2.cloned.1.call-start = ((), (), s32[]{:S(2)}) async-start(), calls=%async_computation.2 | async-start | bytes 131072 | tf_op jit(solution)/shard_map/psum | solution.py:69
Sparse Core Ops, SparseCore 0:
  9.5 53.2 all-gather.1
  335.8 97.3 all-reduce.1
where the time goes:
time: 449 us; the launch traced here: 445 us
  other arithmetic  159 us (35%)
  waiting for transfers between devices  151 us (34%)
  local copies, waits for them, and re-layouts  91.1 us (20%)
  matrix products  23.8 us (5%)
  between operations  13.5 us (3%)
  starting transfers between devices  7.66 us (2%)
    unnamed x1, other arithmetic  157 us
    psum x1, waiting for transfers between devices, on_device(): shrink = lax.psum(combined[:, hidden_width:], 'tensor')  82.1 us
    all_to_all x1, waiting for transfers between devices, on_device(): lax.all_to_all(adapter_up, 'tensor', split_axis=2, concat_axis=0, tiled=T...  67.8 us
    unnamed x15, local copies, waits for them, and re-layouts  59.8 us
    all_to_all x3, local copies, waits for them, and re-layouts, on_device(): lax.all_to_all(adapter_up, 'tensor', split_axis=2, concat_axis=0, tiled=T...  31.2 us
    dot_general x1, matrix products, on_device(): jnp.dot(segment_piece, up_weight, preferred_element_type=jnp.float32)  15.4 us
  transfers between devices with their start and end apart: 3, of which 2 were waited for; matrix products, arithmetic and copies ran while one was open for 59% of the time, Pallas kernels for 0%

commit v1 on v0

v1 whole, which is shorter than its diff:
```python
import jax
import jax.numpy as jnp
from jax import lax
from jax.sharding import PartitionSpec as P

ADAPTER_ALPHA = 32.0


def row_tables(row_count, ranks, adapter_slot, segment_lengths, segment_adapter):
    seg_ends = jnp.cumsum(segment_lengths)
    positions = jnp.arange(row_count, dtype=jnp.int32)
    seg_row = jnp.sum((seg_ends[None, :] <= positions[:, None]).astype(jnp.int32), axis=1)
    seg_pick = (
        seg_row[:, None] == jnp.arange(segment_lengths.shape[0], dtype=jnp.int32)[None, :]
    ).astype(jnp.int32)
    adapter_row = jnp.sum(seg_pick * segment_adapter[None, :], axis=1)
    pool_pick = (
        adapter_row[:, None] == jnp.arange(ranks.shape[0], dtype=jnp.int32)[None, :]
    ).astype(jnp.int32)
    slot_row = jnp.sum(pool_pick * adapter_slot[None, :], axis=1)
    row_rank_values = jnp.sum(pool_pick * ranks[None, :], axis=1)
    return (slot_row, row_rank_values)


def on_device(
    input_rows,
    up_weight,
    adapter_down,
    adapter_up,
    ranks,
    adapter_slot,
    segment_lengths,
    segment_adapter,
):
    shards = lax.axis_size("tensor")
    position = lax.axis_index("tensor")
    total_rows = input_rows.shape[0] * shards
    stored, rank_width, hidden = adapter_up.shape
    width = hidden // shards
    outgoing = jnp.stack(
        [adapter_up[:, :, i * width : (i + 1) * width] for i in range(shards)], axis=0
    )
    incoming = lax.all_to_all(outgoing, "tensor", split_axis=0, concat_axis=0, tiled=True)
    rows = lax.all_gather(input_rows, "tensor", axis=0, tiled=True)
    slot_row, row_rank = row_tables(
        total_rows, ranks, adapter_slot, segment_lengths, segment_adapter
    )
    shrink = jnp.einsum("gf,ojf->ogj", rows, adapter_down, preferred_element_type=jnp.float32)
    own = position * stored + jnp.arange(stored, dtype=jnp.int32)
    inside = jnp.arange(rank_width, dtype=jnp.int32)[None, :] < row_rank[:, None]
    keep = (slot_row[None, :] == own[:, None])[:, :, None] & inside[None]
    scale = ADAPTER_ALPHA / row_rank.astype(jnp.float32)
    own_coeff = jnp.where(keep, shrink * scale[None, :, None], 0.0).astype(jnp.bfloat16)
    coeff = lax.all_gather(own_coeff, "tensor", axis=0, tiled=True)
    base = jnp.dot(rows, up_weight, preferred_element_type=jnp.float32)
    placed = coeff.transpose(1, 0, 2).reshape(total_rows, shards * stored * rank_width)
    factors = incoming.reshape(shards * stored * rank_width, width)
    term = jnp.dot(placed, factors, preferred_element_type=jnp.float32)
    return (base + term).astype(jnp.bfloat16)


def solution(mesh):
    placed = (
        P(("groups", "tensor"), None),
        P(None, "tensor"),
        P(("groups", "tensor"), None, None),
        P(("groups", "tensor"), None, None),
        P("groups"),
        P("groups"),
        P("groups"),
        P("groups"),
    )
    return jax.shard_map(
        on_device, mesh=mesh, in_specs=placed, out_specs=P("groups", "tensor"), check_vma=False
    )
```

time: 449 us -> 172 us (0.38)
  the two profiles are of different devices: /device:TPU:0 before, /device:TPU:9 now
where the time goes in v1:
time: 172 us; the launch traced here: 171 us
  blocking collectives  56.5 us (33%)
  waiting for transfers between devices  46.7 us (27%)
  local copies, waits for them, and re-layouts  26.5 us (15%)
  matrix products  21.2 us (12%)
  between operations  13.4 us (8%)
  starting transfers between devices  6.77 us (4%)
    all_gather x1, blocking collectives, on_device(): coeff = lax.all_gather(own_coeff, 'tensor', axis=0, tiled=True)  56.5 us
    all_gather x1, waiting for transfers between devices, on_device(): rows = lax.all_gather(input_rows, 'tensor', axis=0, tiled=True)  46 us
    unnamed x27, local copies, waits for them, and re-layouts  24.8 us
    dot_general x1, matrix products, on_device(): base = jnp.dot(rows, up_weight, preferred_element_type=jnp.float32)  13.3 us
    all_to_all x1, starting transfers between devices, on_device(): lax.all_to_all(outgoing, 'tensor', split_axis=0, concat_axis=0, tiled=True)  6.77 us
    dot_general x1, matrix products, on_device(): term = jnp.dot(placed, factors, preferred_element_type=jnp.float32)  4.1 us
    dot_general x1, matrix products, on_device(): jnp.einsum('gf,ojf->ogj', rows, adapter_down, preferred_element_type=jnp....  3.73 us
  transfers between devices with their start and end apart: 2, of which 1 were waited for; matrix products, arithmetic and copies ran while one was open for 26% of the time, Pallas kernels for 0%

profile of v1, /device:TPU:9, one launch (start us, length us, event | category | flops | bytes accessed | tf_op | source)
XLA Modules:
  0.0 171.5 jit_solution(65767278873160898)
XLA Ops:
  6.5 0.0 copy-start
  6.5 0.0 all-gather.2.cloned.1.call-start
  6.5 0.7 all-gather.2.cloned.1.call-update
  7.3 1.6 bitcast_dynamic-update-slice_fusion.15
  8.9 1.6 bitcast_dynamic-update-slice_fusion.14
  10.5 1.7 bitcast_dynamic-update-slice_fusion.13
  12.2 1.7 bitcast_dynamic-update-slice_fusion.12
  13.9 1.6 bitcast_dynamic-update-slice_fusion.11
  15.5 1.7 bitcast_dynamic-update-slice_fusion.10
  17.2 1.7 bitcast_dynamic-update-slice_fusion.9
  18.8 1.7 bitcast_dynamic-update-slice_fusion.8
  20.5 1.7 bitcast_dynamic-update-slice_fusion.7
  22.2 1.6 bitcast_dynamic-update-slice_fusion.6
  23.8 1.6 bitcast_dynamic-update-slice_fusion.5
  25.4 1.6 bitcast_dynamic-update-slice_fusion.4
  27.1 1.6 bitcast_dynamic-update-slice_fusion.3
  28.7 1.6 bitcast_dynamic-update-slice_fusion.2
  30.4 1.7 bitcast_dynamic-update-slice_fusion.1
  32.0 1.6 bitcast_dynamic-update-slice_fusion
  33.7 6.8 %all-to-all-start = ((bf16[16,1,64,1792]{3,2,1,0:T(8,128)(2,1)}), bf16[16,1,64,1792]{3,2,1,0:T(8,128)(2,1)}, u32[]{:S(2)}, u32[]{:S(2)}) async-start(bf16[16,1,64,1792]{3,2,1,0:T(8,128)(2,1)} %bitcast_dynamic-update-slice_fusion), calls=%async_computation | async-start | bytes 7340032 | tf_op jit(solution)/shard_map/all_to_all | solution.py:43
  40.4 0.1 copy.12
  40.6 0.1 reduce
  40.7 0.1 convert_reduce_fusion
  40.8 0.1 select_reduce_fusion.2
  40.9 0.1 select_reduce_fusion.1
  41.0 46.0 %all-gather.2.cloned.1.call-done = bf16[256,8192]{1,0:T(8,128)(2,1)} async-done(((bf16[16,8192]{1,0:T(8,128)(2,1)}), bf16[256,8192]{1,0:T(8,128)(2,1)}) %all-gather.2.cloned.1.call-update) | async-done | bytes 4194320 | tf_op jit(solution)/shard_map/all_gather | solution.py:44
  86.9 3.7 %fusion.4 = bf16[1,256,64]{1,2,0:T(8,128)(2,1)S(1)} fusion(bf16[256,8192]{1,0:T(8,128)(2,1)} %all-gather.2.cloned.1.call-done, bf16[1,64,8192]{2,1,0:T(8,128)(2,1)S(1)} %copy-done, f32[256]{0:T(256)S(1)} %convert_divide_fusion, s32[256]{0:T(256)S(1)} %get-tuple-element.6, pred[256]{0:T(512)(128)(4,1)S(1)} %broadcast_compare_fusion), kind=kOutput, calls=%fused_computation.6 | convolution fusion | flops 268517376 | bytes 5277952 | tf_op jit(solution)/shard_map/gf,ojf->ogj/dot_general | solution.py:48
  90.7 56.5 %all_gather.7 = bf16[16,256,64]{1,2,0:T(8,128)(2,1)S(1)} all-gather(bf16[1,256,64]{1,2,0:T(8,128)(2,1)S(1)} %fusion.4), channel_id=1, replica_groups=mesh['groups'=2,'tensor'=16] {'tensor'}, dimensions={0}, use_global_device_ids=true | all-gather | bytes 557056 | tf_op jit(solution)/shard_map/all_gather | solution.py:54
  147.2 0.0 copy-done.1
  147.2 13.3 %fusion.7 = f32[256,1792]{1,0:T(8,128)S(1)} fusion(bf16[256,8192]{1,0:T(8,128)(2,1)S(1)} %copy-done.1, bf16[8192,1792]{1,0:T(8,128)(2,1)} %param.9), kind=kOutput, calls=%fused_computation.35 | convolution fusion | flops 7516192768 | bytes 35389440 | tf_op jit(solution)/shard_map/dot_general | solution.py:55
  160.5 0.0 all-to-all-done
  160.5 4.1 %fusion = bf16[256,1792]{1,0:T(8,128)(2,1)} fusion(f32[256,1792]{1,0:T(8,128)S(1)} %fusion.7, bf16[256,1024]{0,1:T(8,128)(2,1)S(1)} %bitcast.61, bf16[1024,1792]{1,0:T(8,128)(2,1)} %bitcast.22), kind=kOutput, calls=%fused_computation.1 | convolution fusion | flops 940441600 | bytes 6946816 | tf_op jit(solution)/shard_map/dot_general | solution.py:58
  (13 shorter events, 0.1 us)
Async XLA Ops:
  6.5 80.4 %copy-start = (bf16[1,64,8192]{2,1,0:T(8,128)(2,1)S(1)}, bf16[1,64,8192]{2,1,0:T(8,128)(2,1)}, u32[]{:S(2)}) copy-start(bf16[1,64,8192]{2,1,0:T(8,128)(2,1)} %param.10) | copy-start | bytes 3145732
  6.5 80.4 %all-gather.2.cloned.1.call-start = ((), (), s32[]{:S(2)}) async-start(), calls=%async_computation.1 | async-start | bytes 4456448 | tf_op jit(solution)/shard_map/all_gather | solution.py:44
  33.6 6.8 %copy-start.2 = (s32[16]{0:T(128)S(1)}, s32[16]{0:T(128)}, u32[]{:S(2)}) copy-start(s32[16]{0:T(128)} %param.14) | copy-start | bytes 196
  33.6 7.1 %copy-start.3 = (s32[16]{0:T(128)S(1)}, s32[16]{0:T(128)}, u32[]{:S(2)}) copy-start(s32[16]{0:T(128)} %param.15) | copy-start | bytes 196
  33.7 7.2 %copy-start.4 = (s32[16]{0:T(128)S(1)}, s32[16]{0:T(128)}, u32[]{:S(2)}) copy-start(s32[16]{0:T(128)} %param.13) | copy-start | bytes 196
  33.7 7.2 %copy-start.5 = (s32[16]{0:T(128)S(1)}, s32[16]{0:T(128)}, u32[]{:S(2)}) copy-start(s32[16]{0:T(128)} %param.12) | copy-start | bytes 196
  33.7 126.9 %all-to-all-start = ((bf16[16,1,64,1792]{3,2,1,0:T(8,128)(2,1)}), bf16[16,1,64,1792]{3,2,1,0:T(8,128)(2,1)}, u32[]{:S(2)}, u32[]{:S(2)}) async-start(bf16[16,1,64,1792]{3,2,1,0:T(8,128)(2,1)} %bitcast_dynamic-update-slice_fusion), calls=%async_computation | async-start | bytes 7340032 | tf_op jit(solution)/shard_map/all_to_all | solution.py:43
  86.9 60.2 %copy-start.1 = (bf16[256,8192]{1,0:T(8,128)(2,1)S(1)}, bf16[256,8192]{1,0:T(8,128)(2,1)}, u32[]{:S(2)}) copy-start(bf16[256,8192]{1,0:T(8,128)(2,1)} %all-gather.2.cloned.1.call-done) | copy-start | bytes 12582916
Sparse Core Ops, SparseCore 0:
  9.5 77.3 all-gather.1

commit v2 on v1

--- a/solution.py
+++ b/solution.py
@@ -1,6 +1,7 @@
 import jax
 import jax.numpy as jnp
 from jax import lax
+from jax.experimental import pallas as pl
 from jax.sharding import PartitionSpec as P
 
 ADAPTER_ALPHA = 32.0
@@ -22,6 +23,27 @@
     return (slot_row, row_rank_values)
 
 
+def block_copy(source, target):
+    target[0] = source[...]
+
+
+def split_columns(array, shards):
+    stored, rank_width, hidden = array.shape
+    width = hidden // shards
+    if width % 128:
+        return jnp.stack([array[:, :, i * width : (i + 1) * width] for i in range(shards)], axis=0)
+    return pl.pallas_call(
+        block_copy,
+        grid=(shards,),
+        in_specs=[pl.BlockSpec((stored, rank_width, width), lambda i: (0, 0, i))],
+        out_specs=pl.BlockSpec((1, stored, rank_width, width), lambda i: (i, 0, 0, 0)),
+        out_shape=jax.ShapeDtypeStruct((shards, stored, rank_width, width), array.dtype),
+        cost_estimate=pl.CostEstimate(
+            flops=0, bytes_accessed=4 * stored * rank_width * hidden, transcendentals=0
+        ),
+    )(array)
+
+
 def on_device(
     input_rows,
     up_weight,
@@ -37,9 +59,7 @@
     total_rows = input_rows.shape[0] * shards
     stored, rank_width, hidden = adapter_up.shape
     width = hidden // shards
-    outgoing = jnp.stack(
-        [adapter_up[:, :, i * width : (i + 1) * width] for i in range(shards)], axis=0
-    )
+    outgoing = split_columns(adapter_up, shards)
     incoming = lax.all_to_all(outgoing, "tensor", split_axis=0, concat_axis=0, tiled=True)
     rows = lax.all_gather(input_rows, "tensor", axis=0, tiled=True)
     slot_row, row_rank = row_tables(
@@ -51,8 +71,9 @@
     keep = (slot_row[None, :] == own[:, None])[:, :, None] & inside[None]
     scale = ADAPTER_ALPHA / row_rank.astype(jnp.float32)
     own_coeff = jnp.where(keep, shrink * scale[None, :, None], 0.0).astype(jnp.bfloat16)
+    base = jnp.dot(rows, up_weight, preferred_element_type=jnp.float32)
+    own_coeff, base = lax.optimization_barrier((own_coeff, base))
     coeff = lax.all_gather(own_coeff, "tensor", axis=0, tiled=True)
-    base = jnp.dot(rows, up_weight, preferred_element_type=jnp.float32)
     placed = coeff.transpose(1, 0, 2).reshape(total_rows, shards * stored * rank_width)
     factors = incoming.reshape(shards * stored * rank_width, width)
     term = jnp.dot(placed, factors, preferred_element_type=jnp.float32)

time: 172 us -> 158 us (0.919)
  the two profiles are of different devices: /device:TPU:9 before, /device:TPU:0 now
where the time goes in v2:
time: 158 us
  waiting for transfers between devices  84 us (53%)
  matrix products  21.2 us (13%)
  blocking collectives  20.9 us (13%)
  between operations  13.4 us (8%)
  Pallas kernels  10 us (6%)
  starting transfers between devices  7.58 us (5%)
    all_gather x1, waiting for transfers between devices, on_device(): rows = lax.all_gather(input_rows, 'tensor', axis=0, tiled=True)  83.2 us
    all_gather x1, blocking collectives, on_device(): coeff = lax.all_gather(own_coeff, 'tensor', axis=0, tiled=True)  20.9 us
    dot_general x1, matrix products, on_device(): base = jnp.dot(rows, up_weight, preferred_element_type=jnp.float32)  13.3 us
    pallas_call x1, Pallas kernels, split_columns(): pl.pallas_call(block_copy, grid=(shards,), in_specs=[pl.BlockSpec((stored...  10 us
    all_to_all x1, starting transfers between devices, on_device(): lax.all_to_all(outgoing, 'tensor', split_axis=0, concat_axis=0, tiled=True)  7.57 us
    dot_general x1, matrix products, on_device(): term = jnp.dot(placed, factors, preferred_element_type=jnp.float32)  4.1 us
    dot_general x1, matrix products, on_device(): jnp.einsum('gf,ojf->ogj', rows, adapter_down, preferred_element_type=jnp....  3.73 us
  transfers between devices with their start and end apart: 2, of which 1 were waited for; matrix products, arithmetic and copies ran while one was open for 11% of the time, Pallas kernels for 6%

profile of v2, /device:TPU:0, one launch (start us, length us, event | category | flops | bytes accessed | tf_op | source)
XLA Modules:
  0.0 157.6 jit_solution(9088166096151304417)
XLA Ops:
  6.5 0.0 copy-start
  6.5 0.0 all-gather.2.cloned.1.call-start
  6.5 0.7 all-gather.2.cloned.1.call-update
  7.3 10.0 %shard_map.82 = bf16[16,1,64,1792]{3,2,1,0:T(8,128)(2,1)} custom-call(bf16[1,64,28672]{2,1,0:T(8,128)(2,1)} %source.1), custom_call_target="tpu_custom_call" | custom-call | bytes 7340032 | tf_op jit(solution)/shard_map/pallas_call | solution.py:35
  17.3 0.0 copy-start.2
  17.3 0.0 copy-start.3
  17.3 0.0 copy-start.4
  17.3 0.0 copy-start.5
  17.3 7.6 %all-to-all-start = ((bf16[16,1,64,1792]{3,2,1,0:T(8,128)(2,1)}), bf16[16,1,64,1792]{3,2,1,0:T(8,128)(2,1)}, u32[]{:S(2)}, u32[]{:S(2)}) async-start(bf16[16,1,64,1792]{3,2,1,0:T(8,128)(2,1)} %shard_map.82), calls=%async_computation | async-start | bytes 7340032 | tf_op jit(solution)/shard_map/all_to_all | solution.py:63
  24.9 0.0 copy-done.2
  24.9 0.1 copy.12
  25.0 0.1 reduce
  25.1 0.1 convert_reduce_fusion
  25.2 0.0 copy-done.3
  25.2 0.1 select_reduce_fusion.2
  25.3 0.0 copy-done.4
  25.3 0.0 copy-done.5
  25.3 0.1 select_reduce_fusion.1
  25.4 83.2 %all-gather.2.cloned.1.call-done = bf16[256,8192]{1,0:T(8,128)(2,1)} async-done(((bf16[16,8192]{1,0:T(8,128)(2,1)}), bf16[256,8192]{1,0:T(8,128)(2,1)}) %all-gather.2.cloned.1.call-update) | async-done | bytes 4194320 | tf_op jit(solution)/shard_map/all_gather | solution.py:64
  108.7 0.0 copy-done
  108.7 0.0 copy-start.1
  108.7 3.7 %fusion.4 = bf16[1,256,64]{1,2,0:T(8,128)(2,1)S(1)} fusion(bf16[256,8192]{1,0:T(8,128)(2,1)} %all-gather.2.cloned.1.call-done, bf16[1,64,8192]{2,1,0:T(8,128)(2,1)S(1)} %copy-done, f32[256]{0:T(256)S(1)} %convert_divide_fusion, s32[256]{0:T(256)S(1)} %get-tuple-element.10, pred[256]{0:T(512)(128)(4,1)S(1)} %broadcast_compare_fusion), kind=kOutput, calls=%fused_computation.6 | convolution fusion | flops 268517376 | bytes 5277952 | tf_op jit(solution)/shard_map/gf,ojf->ogj/dot_general | solution.py:68
  112.4 0.0 copy-done.1
  112.4 13.3 %fusion.7 = f32[256,1792]{1,0:T(8,128)S(1)} fusion(bf16[256,8192]{1,0:T(8,128)(2,1)S(1)} %copy-done.1, bf16[8192,1792]{1,0:T(8,128)(2,1)} %param.9), kind=kOutput, calls=%fused_computation.19 | convolution fusion | flops 7516192768 | bytes 35389440 | tf_op jit(solution)/shard_map/dot_general | solution.py:74
  125.8 20.9 %all_gather.7 = bf16[16,256,64]{1,2,0:T(8,128)(2,1)S(1)} all-gather(bf16[1,256,64]{1,2,0:T(8,128)(2,1)S(1)} %fusion.4), channel_id=1, replica_groups=mesh['groups'=2,'tensor'=16] {'tensor'}, dimensions={0}, use_global_device_ids=true | all-gather | bytes 557056 | tf_op jit(solution)/shard_map/all_gather | solution.py:76
  146.7 0.0 all-to-all-done
  146.7 4.1 %fusion = bf16[256,1792]{1,0:T(8,128)(2,1)} fusion(f32[256,1792]{1,0:T(8,128)S(1)} %fusion.7, bf16[256,1024]{0,1:T(8,128)(2,1)S(1)} %bitcast.29, bf16[1024,1792]{1,0:T(8,128)(2,1)} %bitcast.6), kind=kOutput, calls=%fused_computation.1 | convolution fusion | flops 940441600 | bytes 6946816 | tf_op jit(solution)/shard_map/dot_general | solution.py:79
  (3 shorter events, 0.0 us)
Async XLA Ops:
  6.5 102.1 %copy-start = (bf16[1,64,8192]{2,1,0:T(8,128)(2,1)S(1)}, bf16[1,64,8192]{2,1,0:T(8,128)(2,1)}, u32[]{:S(2)}) copy-start(bf16[1,64,8192]{2,1,0:T(8,128)(2,1)} %param.10) | copy-start | bytes 3145732
  6.5 102.1 %all-gather.2.cloned.1.call-start = ((), (), s32[]{:S(2)}) async-start(), calls=%async_computation.1 | async-start | bytes 4456448 | tf_op jit(solution)/shard_map/all_gather | solution.py:64
  17.3 7.6 %copy-start.2 = (s32[16]{0:T(128)S(1)}, s32[16]{0:T(128)}, u32[]{:S(2)}) copy-start(s32[16]{0:T(128)} %param.14) | copy-start | bytes 196
  17.3 7.9 %copy-start.3 = (s32[16]{0:T(128)S(1)}, s32[16]{0:T(128)}, u32[]{:S(2)}) copy-start(s32[16]{0:T(128)} %param.15) | copy-start | bytes 196
  17.3 8.0 %copy-start.4 = (s32[16]{0:T(128)S(1)}, s32[16]{0:T(128)}, u32[]{:S(2)}) copy-start(s32[16]{0:T(128)} %param.13) | copy-start | bytes 196
  17.3 8.0 %copy-start.5 = (s32[16]{0:T(128)S(1)}, s32[16]{0:T(128)}, u32[]{:S(2)}) copy-start(s32[16]{0:T(128)} %param.12) | copy-start | bytes 196
  17.3 129.4 %all-to-all-start = ((bf16[16,1,64,1792]{3,2,1,0:T(8,128)(2,1)}), bf16[16,1,64,1792]{3,2,1,0:T(8,128)(2,1)}, u32[]{:S(2)}, u32[]{:S(2)}) async-start(bf16[16,1,64,1792]{3,2,1,0:T(8,128)(2,1)} %shard_map.82), calls=%async_computation | async-start | bytes 7340032 | tf_op jit(solution)/shard_map/all_to_all | solution.py:63
  108.7 3.7 %copy-start.1 = (bf16[256,8192]{1,0:T(8,128)(2,1)S(1)}, bf16[256,8192]{1,0:T(8,128)(2,1)}, u32[]{:S(2)}) copy-start(bf16[256,8192]{1,0:T(8,128)(2,1)} %all-gather.2.cloned.1.call-done) | copy-start | bytes 12582916
Sparse Core Ops, SparseCore 0:
  9.5 99.0 all-gather.1

commit v3 on v2

--- a/solution.py
+++ b/solution.py
@@ -2,9 +2,11 @@
 import jax.numpy as jnp
 from jax import lax
 from jax.experimental import pallas as pl
+from jax.experimental.pallas import tpu as pltpu
 from jax.sharding import PartitionSpec as P
 
 ADAPTER_ALPHA = 32.0
+RING_CHIPS = 8
 
 
 def row_tables(row_count, ranks, adapter_slot, segment_lengths, segment_adapter):
@@ -23,25 +25,109 @@
     return (slot_row, row_rank_values)
 
 
-def block_copy(source, target):
-    target[0] = source[...]
-
-
 def split_columns(array, shards):
     stored, rank_width, hidden = array.shape
     width = hidden // shards
     if width % 128:
         return jnp.stack([array[:, :, i * width : (i + 1) * width] for i in range(shards)], axis=0)
+
+    def kernel(source, target, sems):
+        copies = [
+            pltpu.make_async_copy(
+                source.at[:, :, pl.ds(i * width, width)], target.at[i], sems.at[i]
+            )
+            for i in range(shards)
+        ]
+        for copy in copies:
+            copy.start()
+        for copy in copies:
+            copy.wait()
+
     return pl.pallas_call(
-        block_copy,
-        grid=(shards,),
-        in_specs=[pl.BlockSpec((stored, rank_width, width), lambda i: (0, 0, i))],
-        out_specs=pl.BlockSpec((1, stored, rank_width, width), lambda i: (i, 0, 0, 0)),
+        kernel,
+        in_specs=[pl.BlockSpec(memory_space=pl.ANY)],
+        out_specs=pl.BlockSpec(memory_space=pl.ANY),
         out_shape=jax.ShapeDtypeStruct((shards, stored, rank_width, width), array.dtype),
+        scratch_shapes=[pltpu.SemaphoreType.DMA((shards,))],
         cost_estimate=pl.CostEstimate(
             flops=0, bytes_accessed=4 * stored * rank_width * hidden, transcendentals=0
         ),
     )(array)
+
+
+def place_blocks(blocks, places):
+    count = len(blocks)
+    height, width = blocks[0].shape
+
+    def kernel(places_ref, *refs):
+        sources, target, sems = refs[:count], refs[count], refs[count + 1]
+        copies = [
+            pltpu.make_async_copy(
+                sources[i],
+                target.at[pl.ds(pl.multiple_of(places_ref[i] * height, height), height)],
+                sems.at[i],
+            )
+            for i in range(count)
+        ]
+        for copy in copies:
+            copy.start()
+        for copy in copies:
+            copy.wait()
+
+    return pl.pallas_call(
+        kernel,
+        in_specs=[pl.BlockSpec(memory_space=pltpu.SMEM)]
+        + [pl.BlockSpec(memory_space=pl.ANY)] * count,
+        out_specs=pl.BlockSpec(memory_space=pl.ANY),
+        out_shape=jax.ShapeDtypeStruct((count * height, width), blocks[0].dtype),
+        scratch_shapes=[pltpu.SemaphoreType.DMA((count,))],
+        cost_estimate=pl.CostEstimate(
+            flops=0, bytes_accessed=4 * count * height * width, transcendentals=0
+        ),
+    )(places, *blocks)
+
+
+def ring_gather(block, shards):
+    chips = shards // 2
+    depth = chips // 2
+    cycle = list(range(0, chips, 2)) + list(range(chips - 1, 0, -2))
+    ahead = [
+        (2 * cycle[p] + c, 2 * cycle[(p + 1) % chips] + c) for p in range(chips) for c in range(2)
+    ]
+    back = [(b, a) for a, b in ahead]
+    sibling = [(t, t ^ 1) for t in range(shards)]
+    position = lax.axis_index("tensor")
+    spot = jnp.zeros((), jnp.int32)
+    for p in range(chips):
+        spot = jnp.where(position // 2 == cycle[p], p, spot)
+    held = {0: block}
+    for step in range(1, depth + 1):
+        held[-step] = lax.ppermute(held[1 - step], "tensor", ahead)
+        if step < chips - depth:
+            held[step] = lax.ppermute(held[step - 1], "tensor", back)
+    table = jnp.asarray(cycle, jnp.int32)
+    blocks, places = [], []
+    for offset, piece in held.items():
+        chip = table[(spot + offset) % chips]
+        blocks += [piece, lax.ppermute(piece, "tensor", sibling)]
+        places += [2 * chip + position % 2, 2 * chip + 1 - position % 2]
+    return place_blocks(blocks, jnp.stack(places).astype(jnp.int32))
+
+
+def gather_rows(block, shards):
+    if shards == 2 * RING_CHIPS:
+        return ring_gather(block, shards)
+    return lax.all_gather(block, "tensor", axis=0, tiled=True)
+
+
+def butterfly_sum(value, shards):
+    if shards & (shards - 1):
+        return lax.psum(value, "tensor")
+    bit = 1
+    while bit < shards:
+        value = value + lax.ppermute(value, "tensor", [(t, t ^ bit) for t in range(shards)])
+        bit *= 2
+    return value
 
 
 def on_device(
@@ -59,23 +145,28 @@
     total_rows = input_rows.shape[0] * shards
     stored, rank_width, hidden = adapter_up.shape
     width = hidden // shards
+    slots = shards * stored
     outgoing = split_columns(adapter_up, shards)
     incoming = lax.all_to_all(outgoing, "tensor", split_axis=0, concat_axis=0, tiled=True)
-    rows = lax.all_gather(input_rows, "tensor", axis=0, tiled=True)
+    rows = gather_rows(input_rows, shards)
     slot_row, row_rank = row_tables(
         total_rows, ranks, adapter_slot, segment_lengths, segment_adapter
     )
-    shrink = jnp.einsum("gf,ojf->ogj", rows, adapter_down, preferred_element_type=jnp.float32)
-    own = position * stored + jnp.arange(stored, dtype=jnp.int32)
     inside = jnp.arange(rank_width, dtype=jnp.int32)[None, :] < row_rank[:, None]
-    keep = (slot_row[None, :] == own[:, None])[:, :, None] & inside[None]
     scale = ADAPTER_ALPHA / row_rank.astype(jnp.float32)
-    own_coeff = jnp.where(keep, shrink * scale[None, :, None], 0.0).astype(jnp.bfloat16)
+    own_coeff = jnp.zeros((total_rows, rank_width), jnp.bfloat16)
+    for i in range(stored):
+        shrink = jnp.einsum(
+            "gf,jf->gj", rows, adapter_down[i], preferred_element_type=jnp.float32
+        )
+        keep = (slot_row == position * stored + i)[:, None] & inside
+        own_coeff += jnp.where(keep, shrink * scale[:, None], 0.0).astype(jnp.bfloat16)
+    coeff = butterfly_sum(own_coeff, shards)
     base = jnp.dot(rows, up_weight, preferred_element_type=jnp.float32)
-    own_coeff, base = lax.optimization_barrier((own_coeff, base))
-    coeff = lax.all_gather(own_coeff, "tensor", axis=0, tiled=True)
-    placed = coeff.transpose(1, 0, 2).reshape(total_rows, shards * stored * rank_width)
-    factors = incoming.reshape(shards * stored * rank_width, width)
+    picked = slot_row[:, None] == jnp.arange(slots, dtype=jnp.int32)[None, :]
+    placed = jnp.where(picked[:, :, None], coeff[:, None, :], 0).astype(jnp.bfloat16)
+    placed = placed.reshape(total_rows, slots * rank_width)
+    factors = incoming.reshape(slots * rank_width, width)
     term = jnp.dot(placed, factors, preferred_element_type=jnp.float32)
     return (base + term).astype(jnp.bfloat16)
 

time: 158 us -> 402 us (2.54)
  Pallas kernels: 10 us -> 241 us
  starting transfers between devices: 7.58 us -> 40.5 us
  blocking collectives: 20.9 us -> 0 us
  between operations: 13.4 us -> 5.62 us
  waiting for transfers between devices: 84 us -> 89.9 us
    pallas_call x1 -> x2, Pallas kernels: 10 us -> 241 us  [the longest x1 129 us: place_blocks(): pl.pallas_call(kernel, in_specs=[pl.BlockSpec(memory_space=pltpu.SMEM)] +...]
    ppermute x0 -> x19, waiting for transfers between devices: none -> 89.9 us  [the longest x4 77.3 us: ring_gather(): held[-step] = lax.ppermute(held[1 - step], 'tensor', ahead)]
    all_gather x1 -> x0, waiting for transfers between devices: 83.2 us -> none  [on_device(): rows = lax.all_gather(input_rows, 'tensor', axis=0, tiled=True)]
    ppermute x0 -> x19, starting transfers between devices: none -> 32.9 us  [the longest x4 25.6 us: ring_gather(): held[-step] = lax.ppermute(held[1 - step], 'tensor', ahead)]
    all_gather x1 -> x0, blocking collectives: 20.9 us -> none  [on_device(): coeff = lax.all_gather(own_coeff, 'tensor', axis=0, tiled=True)]
  transfers between devices with their start and end apart: 2 -> 20, of which waited for: 1 -> 9; matrix products, arithmetic and copies ran while one was open for 11% -> 1% of each run, Pallas kernels for 6% -> 32%
where the time goes in v3:
time: 402 us; the launch traced here: 401 us
  Pallas kernels  241 us (60%)
  waiting for transfers between devices  89.9 us (22%)
  starting transfers between devices  40.5 us (10%)
  matrix products  21.3 us (5%)
  between operations  5.62 us (1%)
    pallas_call x1, Pallas kernels, place_blocks(): pl.pallas_call(kernel, in_specs=[pl.BlockSpec(memory_space=pltpu.SMEM)] +...  129 us
    pallas_call x1, Pallas kernels, split_columns(): pl.pallas_call(kernel, in_specs=[pl.BlockSpec(memory_space=pl.ANY)], out_...  112 us
    ppermute x4, waiting for transfers between devices, ring_gather(): held[-step] = lax.ppermute(held[1 - step], 'tensor', ahead)  77.3 us
    ppermute x4, starting transfers between devices, ring_gather(): held[-step] = lax.ppermute(held[1 - step], 'tensor', ahead)  25.6 us
    dot_general x1, matrix products, on_device(): base = jnp.dot(rows, up_weight, preferred_element_type=jnp.float32)  14.4 us
    ppermute x4, waiting for transfers between devices, butterfly_sum(): lax.ppermute(value, 'tensor', [(t, t ^ bit) for t in range(shards)])  10.3 us
  transfers between devices with their start and end apart: 20, of which 9 were waited for; matrix products, arithmetic and copies ran while one was open for 1% of the time, Pallas kernels for 32%

profile of v3, /device:TPU:0, one launch (start us, length us, event | category | flops | bytes accessed | tf_op | source)
XLA Modules:
  0.0 401.3 jit_solution(15950050325174840881)
XLA Ops:
  0.0 112.4 %shard_map.92 = bf16[16,1,64,1792]{3,2,1,0:T(8,128)(2,1)} custom-call(bf16[1,64,28672]{2,1,0:T(8,128)(2,1)} %source.1), custom_call_target="tpu_custom_call" | custom-call | bytes 7340032 | tf_op jit(solution)/shard_map/pallas_call | solution.py:46
  112.5 7.6 %all-to-all-start = ((bf16[16,1,64,1792]{3,2,1,0:T(8,128)(2,1)}), bf16[16,1,64,1792]{3,2,1,0:T(8,128)(2,1)}, u32[]{:S(2)}, u32[]{:S(2)}) async-start(bf16[16,1,64,1792]{3,2,1,0:T(8,128)(2,1)} %shard_map.92), calls=%async_computation | async-start | bytes 7340032 | tf_op jit(solution)/shard_map/all_to_all | solution.py:150
  120.1 1.9 collective-permute-start.1
  122.0 0.2 collective-permute-start.3
  122.2 63.7 %collective-permute-done.1.refs_2_ = bf16[16,8192]{1,0:T(8,128)(2,1)S(1)} collective-permute-done((bf16[16,8192]{1,0:T(8,128)(2,1)S(1)}, bf16[16,8192]{1,0:T(8,128)(2,1)S(1)}, u32[]{:S(2)}, u32[]{:S(2)}) %collective-permute-start.1) | collective-permute-done | bytes 262176 | tf_op jit(solution)/shard_map/ppermute | solution.py:105
  185.9 21.2 %collective-permute-start.5 = (bf16[16,8192]{1,0:T(8,128)(2,1)S(1)}, bf16[16,8192]{1,0:T(8,128)(2,1)S(1)}, u32[]{:S(2)}, u32[]{:S(2)}) collective-permute-start(bf16[16,8192]{1,0:T(8,128)(2,1)S(1)} %collective-permute-done.1.refs_2_), channel_id=1, source_target_pairs={{0,4},{1,5},{4,8},{5,9},{8,12},{9,13},{12,14},{13,15},{14,10},{15,... | collective-permute-start | bytes 786440 | tf_op jit(solution)/shard_map/ppermute | solution.py:105
  207.1 5.4 %collective-permute-done.5.refs_6_ = bf16[16,8192]{1,0:T(8,128)(2,1)S(1)} collective-permute-done((bf16[16,8192]{1,0:T(8,128)(2,1)S(1)}, bf16[16,8192]{1,0:T(8,128)(2,1)S(1)}, u32[]{:S(2)}, u32[]{:S(2)}) %collective-permute-start.5) | collective-permute-done | bytes 262176 | tf_op jit(solution)/shard_map/ppermute | solution.py:105
  212.5 2.5 collective-permute-start.9
  215.1 0.1 reduce
  215.2 0.6 collective-permute-start.2
  215.9 1.7 collective-permute-start.11
  217.6 4.6 %collective-permute-done.9.refs_10_ = bf16[16,8192]{1,0:T(8,128)(2,1)S(1)} collective-permute-done((bf16[16,8192]{1,0:T(8,128)(2,1)S(1)}, bf16[16,8192]{1,0:T(8,128)(2,1)S(1)}, u32[]{:S(2)}, u32[]{:S(2)}) %collective-permute-start.9) | collective-permute-done | bytes 262176 | tf_op jit(solution)/shard_map/ppermute | solution.py:105
  222.4 0.1 select_reduce_fusion
  222.6 0.5 collective-permute-start.8
  223.1 0.1 collective-permute-start.10
  223.1 2.2 collective-permute-done.11.refs_12_
  225.3 3.7 collective-permute-done.13.refs_14_
  229.2 0.7 fusion.5
  235.1 0.6 stack.67.places_ref
  235.8 0.6 copy-done.11
  236.4 129.0 %shard_map.91 = bf16[256,8192]{1,0:T(8,128)(2,1)} custom-call(s32[16]{0:T(128)} %stack.67.places_ref, bf16[16,8192]{1,0:T(8,128)(2,1)} %refs_0_.1, bf16[16,8192]{1,0:T(8,128)(2,1)} %copy-done.8, bf16[16,8192]{1,0:T(8,128)(2,1)} %copy-done.3, bf16[16,8192]{1,0:T(8,128)(2,1)} %copy-done.9, bf16[16,8192]{1,0:T(8,128)(2,1)} %copy-done.4, ...), custom_call_target="tpu_custom_call" | custom-call | bytes 8388608 | tf_op jit(solution)/shard_map/pallas_call | solution.py:77
  365.4 3.6 fusion.2
  369.0 0.4 collective-permute-start.15
  369.4 0.9 collective-permute-done.15
  370.3 1.5 collective-permute-start.16
  371.8 2.5 collective-permute-done.16
  374.3 0.9 collective-permute-start.17
  375.1 3.1 collective-permute-done.17
  378.3 1.4 collective-permute-start.18
  379.6 3.9 collective-permute-done.18
  383.6 3.3 fusion.6
  386.9 14.4 %fusion = bf16[256,1792]{1,0:T(8,128)(2,1)} fusion(f32[256,1792]{1,0:T(8,128)S(1)} %fusion.6, bf16[256,8192]{1,0:T(8,128)(2,1)S(1)} %copy-done.1, bf16[8192,1792]{1,0:T(8,128)(2,1)} %param.10), kind=kOutput, calls=%fused_computation.1 | convolution fusion | flops 7517110272 | bytes 36306944 | tf_op jit(solution)/shard_map/dot_general | solution.py:165
  (63 shorter events, 0.7 us)
Async XLA Ops:
  0.0 365.4 %copy-start = (bf16[1,64,8192]{2,1,0:T(8,128)(2,1)S(1)}, bf16[1,64,8192]{2,1,0:T(8,128)(2,1)}, u32[]{:S(2)}) copy-start(bf16[1,64,8192]{2,1,0:T(8,128)(2,1)} %param.11) | copy-start | bytes 3145732
  112.4 102.5 %copy-start.13 = (s32[16]{0:T(128)S(1)}, s32[16]{0:T(128)}, u32[]{:S(2)}) copy-start(s32[16]{0:T(128)} %param.15) | copy-start | bytes 196
  112.5 109.8 %copy-start.14 = (s32[16]{0:T(128)S(1)}, s32[16]{0:T(128)}, u32[]{:S(2)}) copy-start(s32[16]{0:T(128)} %param.16) | copy-start | bytes 196
  112.5 109.9 %copy-start.15 = (s32[16]{0:T(128)S(1)}, s32[16]{0:T(128)}, u32[]{:S(2)}) copy-start(s32[16]{0:T(128)} %param.13) | copy-start | bytes 196
  112.5 109.9 %copy-start.16 = (s32[16]{0:T(128)S(1)}, s32[16]{0:T(128)}, u32[]{:S(2)}) copy-start(s32[16]{0:T(128)} %param.14) | copy-start | bytes 196
  112.5 116.7 %copy-start.12 = (s32[8]{0:T(128)S(1)}, s32[8]{0:T(128)}, u32[]{:S(2)}) copy-start(s32[8]{0:T(128)} %constant.152.clone) | copy-start | bytes 100
  112.5 271.0 %all-to-all-start = ((bf16[16,1,64,1792]{3,2,1,0:T(8,128)(2,1)}), bf16[16,1,64,1792]{3,2,1,0:T(8,128)(2,1)}, u32[]{:S(2)}, u32[]{:S(2)}) async-start(bf16[16,1,64,1792]{3,2,1,0:T(8,128)(2,1)} %shard_map.92), calls=%async_computation | async-start | bytes 7340032 | tf_op jit(solution)/shard_map/all_to_all | solution.py:150
  120.1 65.8 %collective-permute-start.1 = (bf16[16,8192]{1,0:T(8,128)(2,1)S(1)}, bf16[16,8192]{1,0:T(8,128)(2,1)S(1)}, u32[]{:S(2)}, u32[]{:S(2)}) collective-permute-start(bf16[16,8192]{1,0:T(8,128)(2,1)S(1)} %copy-done.2), channel_id=1, source_target_pairs={{0,4},{1,5},{4,8},{5,9},{8,12},{9,13},{12,14},{13,15},{14,10},{15,... | collective-permute-start | bytes 786440 | tf_op jit(solution)/shard_map/ppermute | solution.py:105
  122.0 85.1 %collective-permute-start.3 = (bf16[16,8192]{1,0:T(8,128)(2,1)S(1)}, bf16[16,8192]{1,0:T(8,128)(2,1)S(1)}, u32[]{:S(2)}, u32[]{:S(2)}) collective-permute-start(bf16[16,8192]{1,0:T(8,128)(2,1)S(1)} %copy-done.2), channel_id=1, source_target_pairs={{4,0},{5,1},{8,4},{9,5},{12,8},{13,9},{14,12},{15,13},{10,14},{11,... | collective-permute-start | bytes 786440 | tf_op jit(solution)/shard_map/ppermute | solution.py:107
  185.9 49.9 %copy-start.3 = (bf16[16,8192]{1,0:T(8,128)(2,1)}, bf16[16,8192]{1,0:T(8,128)(2,1)S(1)}, u32[]{:S(2)}) copy-start(bf16[16,8192]{1,0:T(8,128)(2,1)S(1)} %collective-permute-done.1.refs_2_) | copy-start | bytes 786436
  185.9 26.6 %collective-permute-start.5 = (bf16[16,8192]{1,0:T(8,128)(2,1)S(1)}, bf16[16,8192]{1,0:T(8,128)(2,1)S(1)}, u32[]{:S(2)}, u32[]{:S(2)}) collective-permute-start(bf16[16,8192]{1,0:T(8,128)(2,1)S(1)} %collective-permute-done.1.refs_2_), channel_id=1, source_target_pairs={{0,4},{1,5},{4,8},{5,9},{8,12},{9,13},{12,14},{13,15},{14,10},{15,... | collective-permute-start | bytes 786440 | tf_op jit(solution)/shard_map/ppermute | solution.py:105
  207.1 28.6 %copy-start.4 = (bf16[16,8192]{1,0:T(8,128)(2,1)}, bf16[16,8192]{1,0:T(8,128)(2,1)S(1)}, u32[]{:S(2)}) copy-start(bf16[16,8192]{1,0:T(8,128)(2,1)S(1)} %collective-permute-done.3.refs_4_) | copy-start | bytes 786436
  207.1 8.7 %collective-permute-start.7 = (bf16[16,8192]{1,0:T(8,128)(2,1)S(1)}, bf16[16,8192]{1,0:T(8,128)(2,1)S(1)}, u32[]{:S(2)}, u32[]{:S(2)}) collective-permute-start(bf16[16,8192]{1,0:T(8,128)(2,1)S(1)} %collective-permute-done.3.refs_4_), channel_id=1, source_target_pairs={{4,0},{5,1},{8,4},{9,5},{12,8},{13,9},{14,12},{15,13},{10,14},{11,... | collective-permute-start | bytes 786440 | tf_op jit(solution)/shard_map/ppermute | solution.py:107
  212.5 23.3 %copy-start.5 = (bf16[16,8192]{1,0:T(8,128)(2,1)}, bf16[16,8192]{1,0:T(8,128)(2,1)S(1)}, u32[]{:S(2)}) copy-start(bf16[16,8192]{1,0:T(8,128)(2,1)S(1)} %collective-permute-done.5.refs_6_) | copy-start | bytes 786436
  212.5 9.7 %collective-permute-start.9 = (bf16[16,8192]{1,0:T(8,128)(2,1)S(1)}, bf16[16,8192]{1,0:T(8,128)(2,1)S(1)}, u32[]{:S(2)}, u32[]{:S(2)}) collective-permute-start(bf16[16,8192]{1,0:T(8,128)(2,1)S(1)} %collective-permute-done.5.refs_6_), channel_id=1, source_target_pairs={{0,4},{1,5},{4,8},{5,9},{8,12},{9,13},{12,14},{13,15},{14,10},{15,... | collective-permute-start | bytes 786440 | tf_op jit(solution)/shard_map/ppermute | solution.py:105
  215.0 7.5 %collective-permute-start = (bf16[16,8192]{1,0:T(8,128)(2,1)S(1)}, bf16[16,8192]{1,0:T(8,128)(2,1)S(1)}, u32[]{:S(2)}, u32[]{:S(2)}) collective-permute-start(bf16[16,8192]{1,0:T(8,128)(2,1)S(1)} %copy-done.2), channel_id=1, source_target_pairs={{0,1},{1,0},{2,3},{3,2},{4,5},{5,4},{6,7},{7,6},{8,9},{9,8},{10,11... | collective-permute-start | bytes 786440 | tf_op jit(solution)/shard_map/ppermute | solution.py:112
  215.2 7.3 %collective-permute-start.2 = (bf16[16,8192]{1,0:T(8,128)(2,1)S(1)}, bf16[16,8192]{1,0:T(8,128)(2,1)S(1)}, u32[]{:S(2)}, u32[]{:S(2)}) collective-permute-start(bf16[16,8192]{1,0:T(8,128)(2,1)S(1)} %collective-permute-done.1.refs_2_), channel_id=1, source_target_pairs={{0,1},{1,0},{2,3},{3,2},{4,5},{5,4},{6,7},{7,6},{8,9},{9,8},{10,11... | collective-permute-start | bytes 786440 | tf_op jit(solution)/shard_map/ppermute | solution.py:112
  215.8 7.3 %collective-permute-start.4 = (bf16[16,8192]{1,0:T(8,128)(2,1)S(1)}, bf16[16,8192]{1,0:T(8,128)(2,1)S(1)}, u32[]{:S(2)}, u32[]{:S(2)}) collective-permute-start(bf16[16,8192]{1,0:T(8,128)(2,1)S(1)} %collective-permute-done.3.refs_4_), channel_id=1, source_target_pairs={{0,1},{1,0},{2,3},{3,2},{4,5},{5,4},{6,7},{7,6},{8,9},{9,8},{10,11... | collective-permute-start | bytes 786440 | tf_op jit(solution)/shard_map/ppermute | solution.py:112
  215.9 19.9 %copy-start.6 = (bf16[16,8192]{1,0:T(8,128)(2,1)}, bf16[16,8192]{1,0:T(8,128)(2,1)S(1)}, u32[]{:S(2)}) copy-start(bf16[16,8192]{1,0:T(8,128)(2,1)S(1)} %collective-permute-done.7.refs_8_) | copy-start | bytes 786436
  215.9 9.5 %collective-permute-start.11 = (bf16[16,8192]{1,0:T(8,128)(2,1)S(1)}, bf16[16,8192]{1,0:T(8,128)(2,1)}, u32[]{:S(2)}, u32[]{:S(2)}) collective-permute-start(bf16[16,8192]{1,0:T(8,128)(2,1)S(1)} %collective-permute-done.7.refs_8_), channel_id=1, source_target_pairs={{4,0},{5,1},{8,4},{9,5},{12,8},{13,9},{14,12},{15,13},{10,14},{11,... | collective-permute-start | bytes 786440 | tf_op jit(solution)/shard_map/ppermute | solution.py:107
  222.2 13.6 %copy-start.7 = (bf16[16,8192]{1,0:T(8,128)(2,1)}, bf16[16,8192]{1,0:T(8,128)(2,1)S(1)}, u32[]{:S(2)}) copy-start(bf16[16,8192]{1,0:T(8,128)(2,1)S(1)} %collective-permute-done.9.refs_10_) | copy-start | bytes 786436
  222.2 6.8 %collective-permute-start.13 = (bf16[16,8192]{1,0:T(8,128)(2,1)S(1)}, bf16[16,8192]{1,0:T(8,128)(2,1)}, u32[]{:S(2)}, u32[]{:S(2)}) collective-permute-start(bf16[16,8192]{1,0:T(8,128)(2,1)S(1)} %collective-permute-done.9.refs_10_), channel_id=1, source_target_pairs={{0,4},{1,5},{4,8},{5,9},{8,12},{9,13},{12,14},{13,15},{14,10},{15,... | collective-permute-start | bytes 786440 | tf_op jit(solution)/shard_map/ppermute | solution.py:105
  222.5 13.3 %copy-start.8 = (bf16[16,8192]{1,0:T(8,128)(2,1)}, bf16[16,8192]{1,0:T(8,128)(2,1)S(1)}, u32[]{:S(2)}) copy-start(bf16[16,8192]{1,0:T(8,128)(2,1)S(1)} %collective-permute-done.refs_1_) | copy-start | bytes 786436
  222.5 13.2 %collective-permute-start.6 = (bf16[16,8192]{1,0:T(8,128)(2,1)S(1)}, bf16[16,8192]{1,0:T(8,128)(2,1)S(1)}, u32[]{:S(2)}, u32[]{:S(2)}) collective-permute-start(bf16[16,8192]{1,0:T(8,128)(2,1)S(1)} %collective-permute-done.5.refs_6_), channel_id=1, source_target_pairs={{0,1},{1,0},{2,3},{3,2},{4,5},{5,4},{6,7},{7,6},{8,9},{9,8},{10,11... | collective-permute-start | bytes 786440 | tf_op jit(solution)/shard_map/ppermute | solution.py:112
  222.6 13.1 %collective-permute-start.8 = (bf16[16,8192]{1,0:T(8,128)(2,1)S(1)}, bf16[16,8192]{1,0:T(8,128)(2,1)}, u32[]{:S(2)}, u32[]{:S(2)}) collective-permute-start(bf16[16,8192]{1,0:T(8,128)(2,1)S(1)} %collective-permute-done.7.refs_8_), channel_id=1, source_target_pairs={{0,1},{1,0},{2,3},{3,2},{4,5},{5,4},{6,7},{7,6},{8,9},{9,8},{10,11... | collective-permute-start | bytes 786440 | tf_op jit(solution)/shard_map/ppermute | solution.py:112
  223.1 12.7 %collective-permute-start.10 = (bf16[16,8192]{1,0:T(8,128)(2,1)S(1)}, bf16[16,8192]{1,0:T(8,128)(2,1)}, u32[]{:S(2)}, u32[]{:S(2)}) collective-permute-start(bf16[16,8192]{1,0:T(8,128)(2,1)S(1)} %collective-permute-done.9.refs_10_), channel_id=1, source_target_pairs={{0,1},{1,0},{2,3},{3,2},{4,5},{5,4},{6,7},{7,6},{8,9},{9,8},{10,11... | collective-permute-start | bytes 786440 | tf_op jit(solution)/shard_map/ppermute | solution.py:112
  225.3 10.4 %collective-permute-start.12 = (bf16[16,8192]{1,0:T(8,128)(2,1)}, bf16[16,8192]{1,0:T(8,128)(2,1)}, u32[]{:S(2)}, u32[]{:S(2)}) collective-permute-start(bf16[16,8192]{1,0:T(8,128)(2,1)} %collective-permute-done.11.refs_12_), channel_id=1, source_target_pairs={{0,1},{1,0},{2,3},{3,2},{4,5},{5,4},{6,7},{7,6},{8,9},{9,8},{10,11... | collective-permute-start | bytes 786440 | tf_op jit(solution)/shard_map/ppermute | solution.py:112
  229.0 6.7 %collective-permute-start.14 = (bf16[16,8192]{1,0:T(8,128)(2,1)}, bf16[16,8192]{1,0:T(8,128)(2,1)}, u32[]{:S(2)}, u32[]{:S(2)}) collective-permute-start(bf16[16,8192]{1,0:T(8,128)(2,1)} %collective-permute-done.13.refs_14_), channel_id=1, source_target_pairs={{0,1},{1,0},{2,3},{3,2},{4,5},{5,4},{6,7},{7,6},{8,9},{9,8},{10,11... | collective-permute-start | bytes 786440 | tf_op jit(solution)/shard_map/ppermute | solution.py:112
  369.0 1.3 collective-permute-start.15
  370.3 4.0 collective-permute-start.16
  374.3 4.0 collective-permute-start.17
  378.3 5.2 %collective-permute-start.18 = (bf16[256,64]{0,1:T(8,128)(2,1)S(1)}, bf16[256,64]{0,1:T(8,128)(2,1)S(1)}, u32[]{:S(2)}, u32[]{:S(2)}) collective-permute-start(bf16[256,64]{0,1:T(8,128)(2,1)S(1)} %add.194), channel_id=1, source_target_pairs={{0,8},{1,9},{2,10},{3,11},{4,12},{5,13},{6,14},{7,15},{8,0},{9,1},... | collective-permute-start | bytes 98312 | tf_op jit(solution)/shard_map/ppermute | solution.py:128
  (5 other events, 37.7 us)
